TPU v7x, 32 devices: a whole 2x2x4 slice. The times are simulated.
32 devices in a mesh: bx: 4 (over z), by: 8 (over y, x, core).
Axes of the slice: x: 2, y: 2, z: 4, core: 2. Of those that a mesh axis runs over, the one named last changes fastest.
Arguments:
- right_side: float32 [16, 64, 256, 128], P(None, 'bx', 'by'), may hold values from -14 to 14
- conductivity: float32 [64, 256, 128], P('bx', 'by'), may hold values from 0.5 to 1
Outputs:
- solution_field: float32 [16, 64, 256, 128], P(None, 'bx', 'by')
- residual: float32 [16, 64, 256, 128], P(None, 'bx', 'by')
All inputs are finite; a program needn't handle non-finite values.
Results may differ from a plain program's by a relative error of at most 0.023.
Values sent between devices are 32-bit elements; how exact they have to be, the bound alone decides.
A program may use at most 192 MiB of HBM per device.

v0:
```python
import jax
import jax.numpy as jnp
import numpy as np
from jax import lax
from jax.sharding import PartitionSpec as P

S = 16
STEPS = 4


spectrum_center = 7.0
spectrum_radius = 6.0
face_offsets = ((1, 0, 0), (-1, 0, 0), (0, 1, 0), (0, -1, 0), (0, 0, 1), (0, 0, -1))


def with_halo(shard, sides, width):
    for axis, dim in sides:
        devices, length = (lax.axis_size(axis), shard.shape[dim])
        up = [(i, (i + 1) % devices) for i in range(devices - 1)]
        down = [(j, i) for i, j in up]
        last = lax.slice_in_dim(shard, length - width, length, axis=dim)
        initial = lax.slice_in_dim(shard, 0, width, axis=dim)
        before = lax.ppermute(last, axis, up)
        after = lax.ppermute(initial, axis, down)
        shard = jnp.concatenate([before, shard, after], axis=dim)
    return shard


def neighbour(array, off_x, off_y, off_z):
    size_x, size_y, size_z = array.shape[-3:]
    return array[
        ...,
        1 + off_x : size_x - 1 + off_x,
        1 + off_y : size_y - 1 + off_y,
        1 + off_z : size_z - 1 + off_z,
    ]


def apply_shifted(field_pad, coeff_pad):
    coeff_z = jnp.pad(coeff_pad, ((0, 0), (0, 0), (1, 1)))
    field_z = jnp.pad(field_pad, ((0, 0), (0, 0), (0, 0), (1, 1)))
    center_k = neighbour(coeff_z, 0, 0, 0)
    center_v = neighbour(field_z, 0, 0, 0)
    total = center_v
    for offset in face_offsets:
        other_k = neighbour(coeff_z, *offset)
        denom = center_k + other_k
        inside = denom > 0.0
        face = jnp.where(inside, 2.0 * center_k * other_k / jnp.where(inside, denom, 1.0), 0.0)
        total = total + face * (center_v - neighbour(field_z, *offset))
    return (total - spectrum_center * center_v) / spectrum_radius


def cheb_table():
    table = np.zeros((STEPS + 1, STEPS))
    table[0, 0] = 7.0
    table[1, 0] = 6.0
    for power in range(1, STEPS):
        table[power, power] = 7.0
        table[power - 1, power] = 3.0
        table[power + 1, power] = 3.0
    return np.kron(table, np.eye(S))


def solve_normal(normal, load):
    highest = lax.Precision.HIGHEST
    order = normal.shape[0]
    places = jnp.arange(order, dtype=jnp.int32)

    def chol_step(j, factor):
        pick = (places == j).astype(normal.dtype)
        column = jnp.dot(normal, pick, precision=highest) - jnp.dot(
            factor, jnp.dot(pick, factor, precision=highest), precision=highest
        )
        pivot = jnp.sqrt(jnp.dot(pick, column, precision=highest))
        column = jnp.where(places >= j, column / pivot, 0.0)
        return factor + column[:, None] * pick[None, :]

    factor = lax.fori_loop(0, order, chol_step, jnp.zeros_like(normal))

    def forward_step(j, solved):
        pick = (places == j).astype(normal.dtype)
        row = jnp.dot(pick, factor, precision=highest)
        value = (
            jnp.dot(pick, load, precision=highest) - jnp.dot(row, solved, precision=highest)
        ) / jnp.dot(row, pick, precision=highest)
        return solved + pick[:, None] * value[None, :]

    inner = lax.fori_loop(0, order, forward_step, jnp.zeros_like(load))

    def backward_step(i, solved):
        j = order - 1 - i
        pick = (places == j).astype(normal.dtype)
        row = jnp.dot(factor, pick, precision=highest)
        value = (
            jnp.dot(pick, inner, precision=highest) - jnp.dot(row, solved, precision=highest)
        ) / jnp.dot(row, pick, precision=highest)
        return solved + pick[:, None] * value[None, :]

    return lax.fori_loop(0, order, backward_step, jnp.zeros_like(load))


def small_solve(gram):
    table = jnp.asarray(cheb_table(), gram.dtype)
    highest = lax.Precision.HIGHEST
    normal = jnp.dot(table.T, jnp.dot(gram, table, precision=highest), precision=highest)
    load = jnp.dot(table.T, gram[:, :S], precision=highest)
    coeffs = solve_normal(normal, load)
    return (coeffs, jnp.dot(table, coeffs, precision=highest))


def shards(right_side, conductivity):
    highest = lax.Precision.HIGHEST
    stacked = jnp.concatenate([right_side, conductivity[None]], axis=0)
    near = with_halo(stacked, (("bx", 1), ("by", 2)), 1)
    coeff_pad = near[S]
    blocks = [right_side, apply_shifted(near[:S], coeff_pad)]
    for power in range(1, STEPS):
        field_pad = with_halo(blocks[power], (("bx", 1), ("by", 2)), 1)
        blocks.append(2.0 * apply_shifted(field_pad, coeff_pad) - blocks[power - 1])
    matrix = jnp.stack(blocks).reshape(S * (STEPS + 1), -1)
    local_gram = jnp.dot(matrix, matrix.T, precision=highest)
    gram = lax.psum(local_gram, ("bx", "by"))
    coeffs, combined = small_solve(gram)
    solution_field = jnp.dot(coeffs.T, matrix[: S * STEPS], precision=highest).reshape(
        right_side.shape
    )
    residual = right_side - jnp.dot(combined.T, matrix, precision=highest).reshape(right_side.shape)
    return (solution_field, residual)


def solution(mesh):
    placed = (P(None, "bx", "by", None), P("bx", "by", None))
    return jax.shard_map(
        shards,
        mesh=mesh,
        in_specs=placed,
        out_specs=(P(None, "bx", "by", None), P(None, "bx", "by", None)),
        check_vma=False,
    )
```

profile of v0, /device:TPU:0, one launch (start us, length us, event | category | flops | bytes accessed | tf_op | source)
XLA Modules:
  0.0 716.9 jit_solution(10303298079062954395)
XLA Ops:
  0.7 1.3 pad_maximum_fusion.38
  1.9 5.1 collective-permute-start
  7.0 1.3 collective-permute-start.1
  8.3 4.6 collective-permute-done
  12.9 4.1 collective-permute-done.1
  17.2 1.3 collective-permute-start.2
  18.5 1.3 collective-permute-start.3
  19.8 2.4 constant_dynamic-update-slice_fusion.3
  22.3 1.2 collective-permute-done.3
  24.0 15.1 %select_maximum_fusion.12 = f32[16,18,34,130]{3,2,1,0:T(8,128)} fusion(f32[17,18,1,128]{3,2,1,0:T(1,128)S(1)} %collective-permute-done.3, f32[17,18,1,128]{3,2,1,0:T(1,128)S(1)} %collective-permute-done.2, f32[17,1,32,128]{3,2,1,0:T(8,128)S(1)} %collective-permute-done.1, f32[17,1,32,128]{3,2,1,0:T(8,128)S(1)} %collective-permute-done, ...), kind=kLoop, calls=%fused_computation.80 | loop fusion | flops 17821440 | bytes 10418688 | tf_op jit(solution)/shard_map/concatenate | solution.py:25
  39.1 13.1 %constant_dynamic-update-slice_fusion.2 = (f32[5,16,16,32,128]{4,3,2,1,0:T(8,128)}, f32[16,16,32,128]{3,2,1,0:T(8,128)S(1)}) fusion(f32[5,16,16,32,128]{4,3,2,1,0:T(8,128)} %constant_dynamic-update-slice_fusion.3, f32[16,16,32,128]{3,2,1,0:T(8,128)S(1)} %copy-done, f32[16,18,34,130]{3,2,1,0:T(8,128)} %select_maximum_fusion.12, ...), kind=kLoop, calls=%fused_computation.249 | loop fusion | flops 34603008 | bytes 23676928
  52.2 2.7 fusion.140
  55.0 1.3 collective-permute-start.4
  56.3 4.6 collective-permute-start.5
  60.9 2.4 collective-permute-done.4
  63.3 1.7 collective-permute-done.5
  65.1 1.3 collective-permute-start.6
  66.4 5.5 collective-permute-start.7
  72.7 8.8 %select_maximum_fusion.8 = f32[16,18,34,130]{3,2,1,0:T(8,128)} fusion(f32[16,18,1,128]{3,2,1,0:T(1,128)S(1)} %collective-permute-done.6, f32[16,18,1,128]{3,2,1,0:T(1,128)S(1)} %collective-permute-done.7, f32[16,1,32,128]{3,2,1,0:T(8,128)S(1)} %collective-permute-done.4, f32[16,16,32,128]{3,2,1,0:T(8,128)S(1)} %get-tuple-element.386, ...), kind=kLoop, calls=%fused_computation.76 | loop fusion | flops 15275520 | bytes 10105344 | tf_op jit(solution)/shard_map/concatenate | solution.py:25
  81.5 10.6 %constant_dynamic-update-slice_fusion.1 = (f32[5,16,16,32,128]{4,3,2,1,0:T(8,128)}, f32[16,16,32,128]{3,2,1,0:T(8,128)S(1)}) fusion(f32[5,16,16,32,128]{4,3,2,1,0:T(8,128)} %get-tuple-element.365, f32[16,16,32,128]{3,2,1,0:T(8,128)S(1)} %copy-done, f32[16,16,32,128]{3,2,1,0:T(8,128)S(1)} %get-tuple-element.366, ...), kind=kLoop, calls=%fused_computation.248 | loop fusion | flops 31457280 | bytes 31752192
  92.2 1.3 collective-permute-start.8
  93.5 4.7 collective-permute-start.9
  98.3 2.4 collective-permute-done.8
  100.7 1.7 collective-permute-done.9
  102.6 1.3 collective-permute-start.10
  103.9 5.2 collective-permute-start.11
  109.1 1.0 collective-permute-done.11
  110.1 8.9 %select_maximum_fusion.4 = f32[16,18,34,130]{3,2,1,0:T(8,128)} fusion(f32[16,18,1,128]{3,2,1,0:T(1,128)S(1)} %collective-permute-done.10, f32[16,18,1,128]{3,2,1,0:T(1,128)S(1)} %collective-permute-done.11, f32[16,1,32,128]{3,2,1,0:T(8,128)S(1)} %collective-permute-done.8, f32[16,16,32,128]{3,2,1,0:T(8,128)S(1)} %get-tuple-element.364, ...), kind=kLoop, calls=%fused_computation.72 | loop fusion | flops 15275520 | bytes 10105344 | tf_op jit(solution)/shard_map/concatenate | solution.py:25
  119.0 10.5 %constant_dynamic-update-slice_fusion = (f32[5,16,16,32,128]{4,3,2,1,0:T(8,128)}, f32[16,16,32,128]{3,2,1,0:T(8,128)S(1)}) fusion(f32[5,16,16,32,128]{4,3,2,1,0:T(8,128)} %get-tuple-element.363, f32[16,16,32,128]{3,2,1,0:T(8,128)S(1)} %get-tuple-element.366, f32[16,16,32,128]{3,2,1,0:T(8,128)S(1)} %get-tuple-element.364, ...), kind=kLoop, calls=%fused_computation.247 | loop fusion | flops 32505856 | bytes 27557888
  129.5 2.0 copy-done.4
  131.5 1.3 collective-permute-start.12
  132.8 4.7 collective-permute-start.13
  137.6 2.4 collective-permute-done.12
  139.9 1.5 collective-permute-done.13
  141.4 1.8 pad_maximum_fusion.43
  143.2 1.3 collective-permute-start.14
  144.5 8.8 %collective-permute-start.15 = (f32[16,18,1,128]{3,2,1,0:T(1,128)S(1)}, f32[16,18,1,128]{3,2,1,0:T(1,128)S(1)}, u32[]{:S(2)}, u32[]{:S(2)}) collective-permute-start(f32[16,18,1,128]{3,2,1,0:T(1,128)S(1)} %get-tuple-element.375), channel_id=1, source_target_pairs={{0,1},{1,2},{2,3},{3,4},{4,5},{5,6},{6,7},{8,9},{9,10},{10,11},{11... | collective-permute-start | bytes 442376 | tf_op jit(solution)/shard_map/ppermute | solution.py:23
  153.4 10.9 %pad_maximum_fusion = f32[4,16,16,32,128]{4,3,2,1,0:T(8,128)} fusion(f32[1,16,16,32,128]{4,3,2,1,0:T(8,128)} %bitcast.161, f32[1,16,16,32,128]{4,3,2,1,0:T(8,128)} %bitcast.160, f32[1,16,16,32,128]{4,3,2,1,0:T(8,128)} %get-tuple-element.385, f32[1,16,16,32,128]{4,3,2,1,0:T(8,128)S(1)} %bitcast.159), kind=kLoop, calls=%fused_computation.65 | loop fusion | flops 12582912 | bytes 33554432 | tf_op jit(solution)/shard_map/stack | solution.py:121
  164.3 14.6 %slice.289 = f32[64,65536]{1,0:T(8,128)} reshape(f32[4,16,16,32,128]{4,3,2,1,0:T(8,128)} %pad_maximum_fusion) | data formatting | bytes 33554432 | tf_op jit(solution)/shard_map/slice | solution.py:125
  178.9 14.2 %copy.21 = f32[8,8,512,128]{3,2,1,0:T(8,128)} copy(f32[8,8,512,128]{3,1,2,0:T(8,128)} %bitcast.166) | data formatting | bytes 33554432
  193.1 7.3 %select_maximum_fusion = f32[16,18,34,130]{3,2,1,0:T(8,128)S(1)} fusion(f32[16,18,1,128]{3,2,1,0:T(1,128)S(1)} %collective-permute-done.14, f32[16,18,1,128]{3,2,1,0:T(1,128)S(1)} %collective-permute-done.15, f32[16,1,32,128]{3,2,1,0:T(8,128)S(1)} %collective-permute-done.12, f32[16,16,32,128]{3,2,1,0:T(8,128)S(1)} %copy-done.5, ...), kind=kLoop, calls=%fused_computation.68 | loop fusion | flops 15275520 | bytes 10105344 | tf_op jit(solution)/shard_map/concatenate | solution.py:25
  200.5 9.9 %fusion.59 = f32[5,16,16,32,128]{4,3,2,1,0:T(8,128)} fusion(f32[5,16,16,32,128]{4,3,2,1,0:T(8,128)} %get-tuple-element.361, f32[16,16,32,128]{3,2,1,0:T(8,128)S(1)} %copy-done.3, f32[16,16,32,128]{3,2,1,0:T(8,128)S(1)} %copy-done.5, f32[16,18,34,130]{3,2,1,0:T(8,128)S(1)} %select_maximum_fusion, f32[16,18,1,128]{3,2,1,0:T(1,128)S(1)} %collective-permute-done.15, ...), kind=kLoop, calls=%fused_computation.93 | loop fusion | flops 31457280 | bytes 23363584 | tf_op jit(solution)/shard_map/stack | solution.py:121
  210.4 18.1 %reshape.39 = f32[80,65536]{1,0:T(8,128)} reshape(f32[5,16,16,32,128]{4,3,2,1,0:T(8,128)} %fusion.59) | data formatting | bytes 41943040 | tf_op jit(solution)/shard_map/reshape | solution.py:121
  228.5 23.0 %fusion.147 = f32[80,80]{1,0:T(8,128)S(1)} fusion(f32[80,65536]{1,0:T(8,128)} %reshape.39), kind=kOutput, calls=%fused_computation.256 | convolution fusion | flops 5033164800 | bytes 20997120 | tf_op jit(solution)/shard_map/dot_general | solution.py:122
  251.5 47.0 %psum.7 = f32[80,80]{1,0:T(8,128)S(1)} all-reduce(f32[80,80]{1,0:T(8,128)S(1)} %fusion.147), channel_id=1, replica_groups=mesh['bx'=4,'by'=8] {'bx','by'}, use_global_device_ids=true, to_apply=%region_0.1 | all-reduce | flops 6400 | bytes 51200 | tf_op jit(solution)/shard_map/psum | solution.py:123
  298.9 19.3 %copy.22 = f32[10,8,512,128]{3,2,1,0:T(8,128)} copy(f32[10,8,512,128]{3,1,2,0:T(8,128)} %bitcast.158) | data formatting | bytes 41943040
  318.5 119.9 %while.45 = (s32[]{:T(128)}, f32[64,64]{1,0:T(8,128)S(1)}, f32[64,64]{1,0:T(8,128)S(1)}, s32[]{:T(128)}, s32[]{:T(128)}) while((s32[]{:T(128)}, f32[64,64]{1,0:T(8,128)S(1)}, f32[64,64]{1,0:T(8,128)S(1)}, s32[]{:T(128)}, s32[]{:T(128)}) %tuple.121), condition=%wide.region_2.3_spmd.clone.clone, body=%wide.region_1.2_spmd.clone.clone.sunk | while | flops 168642 | bytes 84589 | solution.py:79
  318.8 0.8 fusion.207
  324.4 0.8 fusion.207
  326.3 0.8 fusion.207
  328.1 0.8 fusion.207
  330.0 0.8 fusion.207
  331.9 0.8 fusion.207
  333.8 0.8 fusion.207
  335.6 0.8 fusion.207
  337.5 0.8 fusion.207
  343.1 0.8 fusion.207
  345.0 0.8 fusion.207
  438.4 110.9 %while.43 = (s32[]{:T(128)}, f32[64,16]{0,1:T(8,128)S(1)}, f32[64,16]{0,1:T(8,128)S(1)}, f32[64,64]{1,0:T(8,128)S(1)}, s32[]{:T(128)}, /*index=5*/s32[]{:T(128)}) while((s32[]{:T(128)}, f32[64,16]{0,1:T(8,128)S(1)}, f32[64,16]{0,1:T(8,128)S(1)}, f32[64,64]{1,0:T(8,128)S(1)}, s32[]{:T(128)}, /*index=5*/s32[]{:T(128)}) %tuple.124), condition=%wide.region_4.5_spmd.clone, body=%wide.region_3.4_spmd.clone.sunk | while | flops 78306 | bytes 34148 | solution.py:89
  549.2 112.1 %while.44 = (s32[]{:T(128)}, f32[64,16]{0,1:T(8,128)S(1)}, f32[64,16]{0,1:T(8,128)S(1)}, f32[64,64]{1,0:T(8,128)S(1)}, s32[]{:T(128)}, /*index=5*/s32[]{:T(128)}, s32[]{:T(128)}) while((s32[]{:T(128)}, f32[64,16]{0,1:T(8,128)S(1)}, f32[64,16]{0,1:T(8,128)S(1)}, f32[64,64]{1,0:T(8,128)S(1)}, s32[]{:T(128)}, /*index=5*/s32[]{:T(128)}, ...), condition=%wide.region_6.7_spmd.clone, body=%wide.region_5.6_spmd.clone.sunk | while | flops 78307 | bytes 34168 | solution.py:100
  661.5 30.3 %copy_subtract_fusion = f32[16,16,32,128]{3,0,2,1:T(8,128)S(1)} fusion(f32[16,16,32,128]{3,2,1,0:T(8,128)} %param.9, f32[16,80,1,1]{1,0,3,2:T(8,128)S(1)} %convolution_bitcast_fusion.7, f32[16,32,128,80]{2,1,0,3:T(8,128)} %bitcast.162), kind=kOutput, calls=%fused_computation.206 | convolution fusion | flops 1007681536 | bytes 29365248 | tf_op jit(solution)/shard_map/dot_general | solution.py:128
  691.9 3.3 copy.12
  695.2 18.0 %fusion.50 = f32[16,16,32,128]{3,0,2,1:T(8,128)S(1)} fusion(f32[16,32,128,64]{2,1,0,3:T(8,128)S(1)} %bitcast.165, f32[64,16]{0,1:T(8,128)S(1)} %get-tuple-element.274), kind=kOutput, calls=%fused_computation.66 | convolution fusion | flops 805306368 | bytes 20975616 | tf_op jit(solution)/shard_map/dot_general | solution.py:125
  713.1 3.3 copy.11
  (1058 shorter events, 289.9 us)
Async XLA Ops:
  0.6 16.4 %copy-start.6 = (f32[16,32,128]{2,1,0:T(8,128)S(1)}, f32[16,32,128]{2,1,0:T(8,128)}, u32[]{:S(2)}) copy-start(f32[16,32,128]{2,1,0:T(8,128)} %param.10) | copy-start | bytes 786436
  0.6 16.4 %copy-start = (f32[16,16,32,128]{3,2,1,0:T(8,128)S(1)}, f32[16,16,32,128]{3,2,1,0:T(8,128)}, u32[]{:S(2)}) copy-start(f32[16,16,32,128]{3,2,1,0:T(8,128)} %param.9) | copy-start | bytes 12582916
  1.9 11.0 %collective-permute-start = (f32[17,1,32,128]{3,2,1,0:T(8,128)S(1)}, f32[17,1,32,128]{3,2,1,0:T(8,128)S(1)}, u32[]{:S(2)}, u32[]{:S(2)}) collective-permute-start(f32[17,1,32,128]{3,2,1,0:T(8,128)S(1)} %get-tuple-element.381), channel_id=1, source_target_pairs={{0,8},{8,16},{16,24},{1,9},{9,17},{17,25},{2,10},{10,18},{18,26},{... | collective-permute-start | bytes 835592 | tf_op jit(solution)/shard_map/ppermute | solution.py:23
  7.0 10.0 %collective-permute-start.1 = (f32[17,1,32,128]{3,2,1,0:T(8,128)S(1)}, f32[17,1,32,128]{3,2,1,0:T(8,128)S(1)}, u32[]{:S(2)}, u32[]{:S(2)}) collective-permute-start(f32[17,1,32,128]{3,2,1,0:T(8,128)S(1)} %get-tuple-element.382), channel_id=1, source_target_pairs={{8,0},{16,8},{24,16},{9,1},{17,9},{25,17},{10,2},{18,10},{26,18},{... | collective-permute-start | bytes 835592 | tf_op jit(solution)/shard_map/ppermute | solution.py:24
  17.2 5.1 collective-permute-start.2
  18.5 5.0 collective-permute-start.3
  55.0 8.3 %collective-permute-start.4 = (f32[16,1,32,128]{3,2,1,0:T(8,128)S(1)}, f32[16,1,32,128]{3,2,1,0:T(8,128)S(1)}, u32[]{:S(2)}, u32[]{:S(2)}) collective-permute-start(f32[16,1,32,128]{3,2,1,0:T(8,128)S(1)} %get-tuple-element.390), channel_id=1, source_target_pairs={{8,0},{16,8},{24,16},{9,1},{17,9},{25,17},{10,2},{18,10},{26,18},{... | collective-permute-start | bytes 786440 | tf_op jit(solution)/shard_map/ppermute | solution.py:24
  56.3 8.6 %collective-permute-start.5 = (f32[16,1,32,128]{3,2,1,0:T(8,128)S(1)}, f32[16,1,32,128]{3,2,1,0:T(8,128)S(1)}, u32[]{:S(2)}, u32[]{:S(2)}) collective-permute-start(f32[16,1,32,128]{3,2,1,0:T(8,128)S(1)} %get-tuple-element.389), channel_id=1, source_target_pairs={{0,8},{8,16},{16,24},{1,9},{9,17},{17,25},{2,10},{10,18},{18,26},{... | collective-permute-start | bytes 786440 | tf_op jit(solution)/shard_map/ppermute | solution.py:23
  65.1 6.8 collective-permute-start.6
  66.4 6.2 collective-permute-start.7
  92.2 26.8 %copy-start.2 = (f32[16,16,32,128]{3,2,1,0:T(8,128)}, f32[16,16,32,128]{3,2,1,0:T(8,128)S(1)}, u32[]{:S(2)}) copy-start(f32[16,16,32,128]{3,2,1,0:T(8,128)S(1)} %get-tuple-element.364) | copy-start | bytes 12582916
  92.2 8.4 %collective-permute-start.8 = (f32[16,1,32,128]{3,2,1,0:T(8,128)S(1)}, f32[16,1,32,128]{3,2,1,0:T(8,128)S(1)}, u32[]{:S(2)}, u32[]{:S(2)}) collective-permute-start(f32[16,1,32,128]{3,2,1,0:T(8,128)S(1)} %get-tuple-element.388), channel_id=1, source_target_pairs={{8,0},{16,8},{24,16},{9,1},{17,9},{25,17},{10,2},{18,10},{26,18},{... | collective-permute-start | bytes 786440 | tf_op jit(solution)/shard_map/ppermute | solution.py:24
  93.5 8.9 %collective-permute-start.9 = (f32[16,1,32,128]{3,2,1,0:T(8,128)S(1)}, f32[16,1,32,128]{3,2,1,0:T(8,128)S(1)}, u32[]{:S(2)}, u32[]{:S(2)}) collective-permute-start(f32[16,1,32,128]{3,2,1,0:T(8,128)S(1)} %get-tuple-element.387), channel_id=1, source_target_pairs={{0,8},{8,16},{16,24},{1,9},{9,17},{17,25},{2,10},{10,18},{18,26},{... | collective-permute-start | bytes 786440 | tf_op jit(solution)/shard_map/ppermute | solution.py:23
  102.6 6.5 collective-permute-start.10
  103.9 6.2 collective-permute-start.11
  129.5 2.0 copy-start.4
  131.5 8.4 %collective-permute-start.12 = (f32[16,1,32,128]{3,2,1,0:T(8,128)S(1)}, f32[16,1,32,128]{3,2,1,0:T(8,128)S(1)}, u32[]{:S(2)}, u32[]{:S(2)}) collective-permute-start(f32[16,1,32,128]{3,2,1,0:T(8,128)S(1)} %get-tuple-element.384), channel_id=1, source_target_pairs={{8,0},{16,8},{24,16},{9,1},{17,9},{25,17},{10,2},{18,10},{26,18},{... | collective-permute-start | bytes 786440 | tf_op jit(solution)/shard_map/ppermute | solution.py:24
  132.8 8.6 %collective-permute-start.13 = (f32[16,1,32,128]{3,2,1,0:T(8,128)S(1)}, f32[16,1,32,128]{3,2,1,0:T(8,128)S(1)}, u32[]{:S(2)}, u32[]{:S(2)}) collective-permute-start(f32[16,1,32,128]{3,2,1,0:T(8,128)S(1)} %get-tuple-element.383), channel_id=1, source_target_pairs={{0,8},{8,16},{16,24},{1,9},{9,17},{17,25},{2,10},{10,18},{18,26},{... | collective-permute-start | bytes 786440 | tf_op jit(solution)/shard_map/ppermute | solution.py:23
  137.6 15.8 %copy-start.1 = (f32[16,16,32,128]{3,2,1,0:T(8,128)S(1)}, f32[16,16,32,128]{3,2,1,0:T(8,128)}, u32[]{:S(2)}) copy-start(f32[16,16,32,128]{3,2,1,0:T(8,128)} %param.9) | copy-start | bytes 12582916
  143.2 49.9 %collective-permute-start.14 = (f32[16,18,1,128]{3,2,1,0:T(1,128)S(1)}, f32[16,18,1,128]{3,2,1,0:T(1,128)S(1)}, u32[]{:S(2)}, u32[]{:S(2)}) collective-permute-start(f32[16,18,1,128]{3,2,1,0:T(1,128)S(1)} %get-tuple-element.376), channel_id=1, source_target_pairs={{1,0},{2,1},{3,2},{4,3},{5,4},{6,5},{7,6},{9,8},{10,9},{11,10},{12... | collective-permute-start | bytes 442376 | tf_op jit(solution)/shard_map/ppermute | solution.py:24
  144.5 48.6 %collective-permute-start.15 = (f32[16,18,1,128]{3,2,1,0:T(1,128)S(1)}, f32[16,18,1,128]{3,2,1,0:T(1,128)S(1)}, u32[]{:S(2)}, u32[]{:S(2)}) collective-permute-start(f32[16,18,1,128]{3,2,1,0:T(1,128)S(1)} %get-tuple-element.375), channel_id=1, source_target_pairs={{0,1},{1,2},{2,3},{3,4},{4,5},{5,6},{6,7},{8,9},{9,10},{10,11},{11... | collective-permute-start | bytes 442376 | tf_op jit(solution)/shard_map/ppermute | solution.py:23
  178.9 14.3 %copy-start.5 = (f32[16,16,32,128]{3,2,1,0:T(8,128)S(1)}, f32[16,16,32,128]{3,2,1,0:T(8,128)}, u32[]{:S(2)}) copy-start(f32[16,16,32,128]{3,2,1,0:T(8,128)} %copy-done.4) | copy-start | bytes 12582916
  193.1 7.3 %copy-start.3 = (f32[16,16,32,128]{3,2,1,0:T(8,128)S(1)}, f32[16,16,32,128]{3,2,1,0:T(8,128)}, u32[]{:S(2)}) copy-start(f32[16,16,32,128]{3,2,1,0:T(8,128)} %copy-done.2) | copy-start | bytes 12582916
  228.5 70.0 %copy-start.7 = (f32[80,64]{1,0:T(8,128)S(1)}, f32[80,64]{1,0:T(8,128)}, u32[]{:S(2)}) copy-start(f32[80,64]{1,0:T(8,128)} %constant.71.clone) | copy-start | bytes 61444
  661.5 33.7 %slice-start = ((s8[16777216]{0:T(1024)(128)(4,1)}), s8[4194304]{0:T(1024)(128)(4,1)S(1)}, s32[]{:S(2)}) async-start(s8[16777216]{0:T(1024)(128)(4,1)} %bitcast.163), calls=%async_computation | async-start | bytes 8388608
  661.5 33.7 %slice-start.1 = ((s8[16777216]{0:T(1024)(128)(4,1)}), s8[4194304]{0:T(1024)(128)(4,1)S(1)}, s32[]{:S(2)}) async-start(s8[16777216]{0:T(1024)(128)(4,1)} %bitcast.163), calls=%async_computation.1 | async-start | bytes 8388608
  661.5 33.6 %slice-start.2 = ((s8[16777216]{0:T(1024)(128)(4,1)}), s8[4194304]{0:T(1024)(128)(4,1)S(1)}, s32[]{:S(2)}) async-start(s8[16777216]{0:T(1024)(128)(4,1)} %bitcast.163), calls=%async_computation.2 | async-start | bytes 8388608
  661.5 33.6 %slice-start.3 = ((s8[16777216]{0:T(1024)(128)(4,1)}), s8[4194304]{0:T(1024)(128)(4,1)S(1)}, s32[]{:S(2)}) async-start(s8[16777216]{0:T(1024)(128)(4,1)} %bitcast.163), calls=%async_computation.3 | async-start | bytes 8388608
where the time goes:
time: 729 us; the launch traced here: 717 us
  matrix products  352 us (48%)
  other arithmetic  118 us (16%)
  local copies, waits for them, and re-layouts  77.5 us (11%)
  starting transfers between devices  50.2 us (7%)
  blocking collectives  47 us (6%)
  loops' own time  46.7 us (6%)
  waiting for transfers between devices  23.7 us (3%)
    dot_general x64, matrix products, chol_step(): jnp.dot(factor, jnp.dot(pick, factor, precision=highest), precision=highest)  52.2 us
    dot_general x64, matrix products, backward_step(): jnp.dot(row, solved, precision=highest)  50.3 us
    dot_general x64, matrix products, forward_step(): jnp.dot(row, solved, precision=highest)  50.3 us
    dot_general x64, matrix products, backward_step(): row = jnp.dot(factor, pick, precision=highest)  48.6 us
    dot_general x64, matrix products, forward_step(): row = jnp.dot(pick, factor, precision=highest)  47.3 us
    psum x1, blocking collectives, shards(): gram = lax.psum(local_gram, ('bx', 'by'))  47 us
    another operation x1, loops' own time, solve_normal(): factor = lax.fori_loop(0, order, chol_step, jnp.zeros_like(normal))  45.5 us
    unnamed x29, local copies, waits for them, and re-layouts  44.7 us
  transfers between devices with their start and end apart: 16, of which 11 were waited for; matrix products, arithmetic and copies ran while one was open for 6% of the time, Pallas kernels for 0%

commit v1 on v0

v1 whole, which is shorter than its diff:
```python
import functools

import jax
import jax.numpy as jnp
import numpy as np
from jax import lax
from jax.experimental import pallas as pl
from jax.experimental.pallas import tpu as pltpu
from jax.sharding import PartitionSpec as P

S = 16
STEPS = 4
MESH = pl.DeviceIdType.MESH


def cheb_small():
    table = np.zeros((STEPS + 1, STEPS))
    table[0, 0] = 7.0
    table[1, 0] = 6.0
    for power in range(1, STEPS):
        table[power, power] = 7.0
        table[power - 1, power] = 3.0
        table[power + 1, power] = 3.0
    return table


def split(a):
    hi = a.astype(jnp.bfloat16)
    lo = (a - hi.astype(jnp.float32)).astype(jnp.bfloat16)
    return hi, lo


def basis_kernel(
    nbx, nby, X, Y, rhs, k_ref, w_out, g_out,
    v, kp, cx, cy, czm, czp, cd, gl, r1, r2,
    in_sem, out_sem, k_send, k_recv, h_send, h_recv, a_send, a_recv, b_send, b_recv,
):
    bx, by = lax.axis_index("bx"), lax.axis_index("by")
    barrier = pltpu.get_barrier_semaphore()

    loads = [
        pltpu.make_async_copy(rhs.at[s], v.at[0, pl.ds(1, X), pl.ds(1, Y), s], in_sem.at[s])
        for s in range(S)
    ]
    for c in loads:
        c.start()
    for d in range(1, nbx):
        pl.semaphore_signal(barrier, inc=1, device_id=(lax.rem(bx + d, nbx), by), device_id_type=MESH)
    for d in range(1, nby):
        pl.semaphore_signal(barrier, inc=1, device_id=(bx, lax.rem(by + d, nby)), device_id_type=MESH)

    @pl.loop(0, X)
    def _(x):
        kp[x + 1, pl.ds(1, Y)] = k_ref[x]

    edges = (bx > 0, bx < nbx - 1, by > 0, by < nby - 1)

    def zero_side(side):
        if side < 2:
            at = 0 if side == 0 else X + 1
            kp[at] = jnp.zeros_like(kp[at])
            for j in range(STEPS):
                @pl.loop(0, Y + 2)
                def _(y):
                    v[j, at, y] = jnp.zeros((S, 128), jnp.float32)
        else:
            at = 0 if side == 2 else Y + 1
            @pl.loop(1, X + 1)
            def _(x):
                kp[x, at] = jnp.zeros((1, 128), jnp.float32)
                for j in range(STEPS):
                    v[j, x, at] = jnp.zeros((S, 128), jnp.float32)

    for side in range(4):
        pl.when(jnp.logical_not(edges[side]))(functools.partial(zero_side, side))
    pl.semaphore_wait(barrier, nbx - 1 + nby - 1)

    targets = ((bx - 1, by), (bx + 1, by), (bx, by - 1), (bx, by + 1))

    def face_copies(ref, send, recv, side):
        xs, ys = pl.ds(1, X), pl.ds(1, Y)
        src, dst = (
            (ref.at[1, ys], ref.at[X + 1, ys]),
            (ref.at[X, ys], ref.at[0, ys]),
            (ref.at[xs, 1], ref.at[xs, Y + 1]),
            (ref.at[xs, Y], ref.at[xs, 0]),
        )[side]
        return pltpu.make_async_remote_copy(
            src_ref=src, dst_ref=dst, send_sem=send.at[side], recv_sem=recv.at[side],
            device_id=targets[side], device_id_type=MESH,
        )

    def start_faces(ref, send, recv):
        for side in range(4):
            @pl.when(edges[side])
            def _(side=side):
                face_copies(ref, send, recv, side).start()

    def wait_recv(ref, send, recv):
        for side in range(4):
            @pl.when(edges[side])
            def _(side=side):
                face_copies(ref, send, recv, side ^ 1).wait_recv()

    def wait_send(ref, send, recv):
        for side in range(4):
            @pl.when(edges[side])
            def _(side=side):
                face_copies(ref, send, recv, side).wait_send()

    start_faces(kp, k_send, k_recv)
    for c in loads:
        c.wait()
    start_faces(v.at[0], h_send.at[0], h_recv.at[0])
    stores = [
        pltpu.make_async_copy(
            v.at[j, pl.ds(1, X), pl.ds(1, Y)], w_out.at[j], out_sem.at[j])
        for j in range(STEPS + 1)
    ]
    stores[0].start()
    wait_recv(kp, k_send, k_recv)

    def face(a, b):
        return (2.0 * a * b) / (a + b)

    third = -1.0 / 3.0

    def coeff_x(x, n, y0):
        cx[x, pl.ds(y0, n)] = third * face(kp[x, pl.ds(y0, n)], kp[x + 1, pl.ds(y0, n)])

    @pl.loop(0, X + 1)
    def _(x):
        coeff_x(x, Y, 1)

    lane = lax.broadcasted_iota(jnp.int32, (Y, 1, 128), 2)

    @pl.loop(1, X + 1)
    def _(x):
        k = kp[x, pl.ds(1, Y)]
        cy[x, pl.ds(1, Y)] = third * face(k, kp[x, pl.ds(2, Y)])
        cy[x, pl.ds(0, 1)] = third * face(kp[x, pl.ds(0, 1)], kp[x, pl.ds(1, 1)])
        up = jnp.where(lane == 127, 0.0, pltpu.roll(k, 127, 2))
        zp = third * face(k, up)
        zm = pltpu.roll(zp, 1, 2)
        czp[x, pl.ds(1, Y)] = zp
        czm[x, pl.ds(1, Y)] = zm
        total = cx[x - 1, pl.ds(1, Y)] + cx[x, pl.ds(1, Y)]
        total = total + cy[x, pl.ds(0, Y)] + cy[x, pl.ds(1, Y)] + zp + zm
        cd[x, pl.ds(1, Y)] = -total - 2.0

    def stencil(j, x, y0, n):
        ys = pl.ds(y0, n)
        c = v[j, x, ys]
        shape = c.shape

        def wide(a):
            return jnp.broadcast_to(a, shape)

        out = wide(cd[x, ys]) * c
        out = out + wide(czp[x, ys]) * pltpu.roll(c, 127, 2)
        out = out + wide(czm[x, ys]) * pltpu.roll(c, 1, 2)
        out = out + wide(cx[x - 1, ys]) * v[j, x - 1, ys]
        out = out + wide(cx[x, ys]) * v[j, x + 1, ys]
        out = out + wide(cy[x, pl.ds(y0 - 1, n)]) * v[j, x, pl.ds(y0 - 1, n)]
        out = out + wide(cy[x, ys]) * v[j, x, pl.ds(y0 + 1, n)]
        if j == 0:
            v[1, x, ys] = 0.5 * out
        else:
            v[j + 1, x, ys] = out - v[j - 1, x, ys]

    CH = 4

    def rows(j, x, lo, hi):
        count = (hi - lo) // CH

        @pl.loop(0, count)
        def _(i):
            stencil(j, x, lo + i * CH, CH)
        if (hi - lo) % CH:
            stencil(j, x, lo + count * CH, (hi - lo) % CH)

    def boundary(j):
        rows(j, 1, 1, Y + 1)
        rows(j, X, 1, Y + 1)

        @pl.loop(2, X)
        def _(x):
            stencil(j, x, 1, 1)
            stencil(j, x, Y, 1)

    def interior(j):
        @pl.loop(2, X)
        def _(x):
            rows(j, x, 2, Y)

    def flat(j, x):
        return jnp.concatenate([v[j, x, 1 + y] for y in range(Y)], axis=1)

    def gram(j):
        def body(x, total):
            hi, lo = split(flat(j, x))
            right = jnp.concatenate([hi, lo], axis=0)
            left = right
            if j > 0:
                phi, plo = split(flat(j - 1, x))
                left = jnp.concatenate([hi, lo, phi, plo], axis=0)
            return total + lax.dot_general(
                left, right, (((1,), (1,)), ((), ())), preferred_element_type=jnp.float32)

        n = 32 if j == 0 else 64
        total = lax.fori_loop(1, X + 1, body, jnp.zeros((n, 32), jnp.float32))
        cols = total[:, :16] + total[:, 16:]
        same = cols[0:16] + cols[16:32]
        gl[0:16, 16 * j:16 * j + 16] = same
        if j > 0:
            gl[16:32, 16 * j:16 * j + 16] = cols[32:48] + cols[48:64]

    gl[...] = jnp.zeros_like(gl)
    gram(0)
    for j in range(STEPS):
        wait_recv(v.at[j], h_send.at[j], h_recv.at[j])
        boundary(j)
        if j + 1 < STEPS:
            start_faces(v.at[j + 1], h_send.at[j + 1], h_recv.at[j + 1])
        interior(j)
        stores[j + 1].start()
        gram(j + 1)

    def spread(axis_at, n, own, src, slots, send, recv):
        copies = []
        for d in range(1, n):
            to = (lax.rem(bx + d, n), by) if axis_at == 0 else (bx, lax.rem(by + d, n))
            copies.append(pltpu.make_async_remote_copy(
                src_ref=src, dst_ref=slots.at[d], send_sem=send.at[d], recv_sem=recv.at[d],
                device_id=to, device_id_type=MESH))
        for c in copies:
            c.start()
        total = src[...]
        for d in range(1, n):
            copies[d - 1].wait_recv()
            total = total + slots[d]
        for c in copies:
            c.wait_send()
        return total

    gl2 = r1.at[0]
    gl2[...] = spread(0, nbx, bx, gl, r1, a_send, a_recv)
    g_out[...] = spread(1, nby, by, gl2, r2, b_send, b_recv)

    wait_send(kp, k_send, k_recv)
    for j in range(STEPS):
        wait_send(v.at[j], h_send.at[j], h_recv.at[j])
    for c in stores:
        c.wait()


def solve(g):
    table = cheb_small()
    same = [g[0:16, 16 * j:16 * j + 16] for j in range(STEPS + 1)]
    cross = [None] + [g[16:32, 16 * j:16 * j + 16] for j in range(1, STEPS + 1)]
    moment = [same[0], cross[1]]
    for k in range(1, STEPS + 1):
        moment.append(2.0 * same[k] - same[0])
        if k < STEPS:
            moment.append(2.0 * cross[k + 1] - cross[1])

    def weighted(weights):
        out = None
        for m, w in zip(moment, weights):
            if w != 0.0:
                out = w * m if out is None else out + w * m
        return out

    rows = []
    for i in range(STEPS):
        blocks = []
        for j in range(STEPS):
            weights = np.zeros(2 * STEPS + 1)
            for a in range(STEPS + 1):
                for b in range(STEPS + 1):
                    w = 0.5 * table[a, i] * table[b, j]
                    weights[a + b] += w
                    weights[abs(a - b)] += w
            blocks.append(weighted([float(w) for w in weights]))
        blocks.append(weighted([float(w) for w in table[:, i]] + [0.0] * STEPS))
        blocks.append(jnp.zeros((16, 48), jnp.float32))
        rows.append(jnp.concatenate(blocks, axis=1))
    a = jnp.concatenate(rows, axis=0)
    order = S * STEPS
    place = lax.broadcasted_iota(jnp.int32, (order, 128), 0)
    for p in range(order):
        col = jnp.broadcast_to(a[:, p:p + 1], (order, 128))
        row = jnp.broadcast_to(a[p:p + 1] / col[p:p + 1], (order, 128))
        a = jnp.where(place == p, row, a - col * row)
    coeffs = [a[16 * i:16 * i + 16, order:order + 16] for i in range(STEPS)]
    zero = jnp.zeros((16, 16), jnp.float32)
    eye = jnp.where(
        lax.broadcasted_iota(jnp.int32, (16, 16), 0) == lax.broadcasted_iota(jnp.int32, (16, 16), 1),
        1.0, 0.0)
    parts = []
    for r in range(STEPS + 1):
        rest = eye if r == 0 else zero
        for i in range(STEPS):
            if table[r, i] != 0.0:
                rest = rest - float(table[r, i]) * coeffs[i]
        first = coeffs[r] if r < STEPS else zero
        parts.append(jnp.concatenate([first, rest, jnp.zeros((16, 96), jnp.float32)], axis=1))
    c = jnp.concatenate(parts, axis=0)
    hi = c.astype(jnp.bfloat16).astype(jnp.float32)
    lo = c - hi
    return jnp.concatenate([hi, hi, lo, jnp.zeros((16, 128), jnp.float32)], axis=0)


def combine_kernel(Y, g_ref, w_ref, sol_ref, res_ref, c_ref):
    @pl.when(pl.program_id(0) == 0)
    def _():
        stacked = solve(g_ref[...])
        c_ref[...] = stacked.T[0:32].astype(jnp.bfloat16)

    CH = 8

    @pl.loop(0, Y // CH)
    def _(t):
        y0 = pl.multiple_of(t * CH, CH)
        cols = []
        for y in range(CH):
            his, los = [], []
            for j in range(STEPS + 1):
                hi, lo = split(w_ref[j, 0, y0 + y])
                his.append(hi)
                los.append(lo)
            cols.append(jnp.concatenate(
                his + los + his + [jnp.zeros((16, 128), jnp.bfloat16)], axis=0))
        right = jnp.concatenate(cols, axis=1)
        out = jnp.dot(c_ref[...], right, preferred_element_type=jnp.float32)
        out = jnp.stack([out[:, 128 * y:128 * y + 128] for y in range(CH)], axis=0)
        out = jnp.swapaxes(out, 0, 1)
        sol_ref[:, 0, pl.ds(y0, CH)] = out[0:16]
        res_ref[:, 0, pl.ds(y0, CH)] = out[16:32]


def shards(right_side, conductivity):
    nbx, nby = lax.axis_size("bx"), lax.axis_size("by")
    X, Y, Z = conductivity.shape
    f32 = jnp.float32
    dma = pltpu.SemaphoreType.DMA
    w, g = pl.pallas_call(
        functools.partial(basis_kernel, nbx, nby, X, Y),
        out_shape=(
            jax.ShapeDtypeStruct((STEPS + 1, X, Y, S, Z), f32),
            jax.ShapeDtypeStruct((32, 128), f32),
        ),
        in_specs=[pl.BlockSpec(memory_space=pl.ANY), pl.BlockSpec(memory_space=pltpu.VMEM)],
        out_specs=(pl.BlockSpec(memory_space=pl.ANY), pl.BlockSpec(memory_space=pltpu.VMEM)),
        scratch_shapes=[
            pltpu.VMEM((STEPS + 1, X + 2, Y + 2, S, Z), f32),
            pltpu.VMEM((X + 2, Y + 2, 1, Z), f32),
            pltpu.VMEM((X + 2, Y + 2, 1, Z), f32),
            pltpu.VMEM((X + 2, Y + 2, 1, Z), f32),
            pltpu.VMEM((X + 2, Y + 2, 1, Z), f32),
            pltpu.VMEM((X + 2, Y + 2, 1, Z), f32),
            pltpu.VMEM((X + 2, Y + 2, 1, Z), f32),
            pltpu.VMEM((32, 128), f32),
            pltpu.VMEM((nbx, 32, 128), f32),
            pltpu.VMEM((nby, 32, 128), f32),
            dma((S,)), dma((STEPS + 1,)), dma((4,)), dma((4,)),
            dma((STEPS, 4)), dma((STEPS, 4)),
            dma((nbx,)), dma((nbx,)), dma((nby,)), dma((nby,)),
        ],
        compiler_params=pltpu.CompilerParams(
            collective_id=0, has_side_effects=True, vmem_limit_bytes=56 * 1024 * 1024),
        name="basis",
    )(right_side, conductivity.reshape(X, Y, 1, Z))
    out = jax.ShapeDtypeStruct((S, X, Y, Z), f32)
    return pl.pallas_call(
        functools.partial(combine_kernel, Y),
        grid=(X,),
        out_shape=(out, out),
        in_specs=[
            pl.BlockSpec((32, 128), lambda x: (0, 0)),
            pl.BlockSpec((STEPS + 1, 1, Y, S, Z), lambda x: (0, x, 0, 0, 0)),
        ],
        out_specs=(
            pl.BlockSpec((S, 1, Y, Z), lambda x: (0, x, 0, 0)),
            pl.BlockSpec((S, 1, Y, Z), lambda x: (0, x, 0, 0)),
        ),
        scratch_shapes=[pltpu.VMEM((32, 256), jnp.bfloat16)],
        compiler_params=pltpu.CompilerParams(vmem_limit_bytes=32 * 1024 * 1024),
        name="combine",
    )(g, w)


def solution(mesh):
    placed = (P(None, "bx", "by", None), P("bx", "by", None))
    return jax.shard_map(
        shards,
        mesh=mesh,
        in_specs=placed,
        out_specs=(P(None, "bx", "by", None), P(None, "bx", "by", None)),
        check_vma=False,
    )
```

time: 729 us -> 125 us (0.17); the launches traced: 717 us -> 125 us
  matrix products: 352 us -> 0 us
  other arithmetic: 118 us -> 0 us
  Pallas kernels: 0 us -> 116 us
  local copies, waits for them, and re-layouts: 77.5 us -> 7.67 us
  starting transfers between devices: 50.2 us -> 0 us
  blocking collectives: 47 us -> 0 us
  loops' own time: 46.7 us -> 0 us
  waiting for transfers between devices: 23.7 us -> 0 us
    dot_general x583 -> x0, matrix products: 352 us -> none  [the longest x64 52.2 us: chol_step(): jnp.dot(factor, jnp.dot(pick, factor, precision=highest), precision=highest)]
    pallas_call x0 -> x2, Pallas kernels: none -> 116 us  [the longest x1 94.4 us: shards(): pl.pallas_call(functools.partial(basis_kernel, nbx, nby, X, Y), out_shape...]
    ppermute x16 -> x0, starting transfers between devices: 50.2 us -> none  [the longest x8 39.9 us: with_halo(): before = lax.ppermute(last, axis, up)]
    psum x1 -> x0, blocking collectives: 47 us -> none  [shards(): gram = lax.psum(local_gram, ('bx', 'by'))]
    another operation x3 -> x0, loops' own time: 46.7 us -> none  [the longest x1 45.5 us: solve_normal(): factor = lax.fori_loop(0, order, chol_step, jnp.zeros_like(normal))]
    concatenate x7 -> x0, other arithmetic: 42.3 us -> none  [with_halo(): shard = jnp.concatenate([before, shard, after], axis=dim)]
    unnamed x29 -> x4, local copies, waits for them, and re-layouts: 44.7 us -> 7.67 us
    unnamed x7 -> x0, other arithmetic: 34.2 us -> none
  transfers between devices with their start and end apart: 16 -> 0, of which waited for: 11 -> 0; matrix products, arithmetic and copies ran while one was open for 6% -> 0% of each run, Pallas kernels for 0% -> 0%
where the time goes in v1:
time: 125 us
  Pallas kernels  116 us (93%)
  local copies, waits for them, and re-layouts  7.67 us (6%)
    pallas_call x1, Pallas kernels, shards(): pl.pallas_call(functools.partial(basis_kernel, nbx, nby, X, Y), out_shape...  94.4 us
    pallas_call x1, Pallas kernels, shards(): pl.pallas_call(functools.partial(combine_kernel, Y), grid=(X,), out_shape...  22.1 us
    unnamed x4, local copies, waits for them, and re-layouts  7.67 us

profile of v1, /device:TPU:0, one launch (start us, length us, event | category | flops | bytes accessed | tf_op | source)
XLA Modules:
  0.0 124.8 jit_solution(11463530163912645981)
XLA Ops:
  0.6 94.4 %basis.1 = (f32[5,16,32,16,128]{4,3,2,1,0:T(8,128)}, f32[32,128]{1,0:T(8,128)}) custom-call(f32[16,16,32,128]{3,2,1,0:T(8,128)} %rhs.1, f32[16,32,1,128]{3,2,1,0:T(1,128)} %bitcast.1), custom_call_target="tpu_custom_call" | custom-call | tf_op jit(solution)/shard_map/basis/pallas_call | solution.py:347
  95.0 0.0 copy-start
  95.1 7.0 %copy-done = f32[5,16,32,16,128]{4,3,2,1,0:T(8,128)S(1)} copy-done((f32[5,16,32,16,128]{4,3,2,1,0:T(8,128)S(1)}, f32[5,16,32,16,128]{4,3,2,1,0:T(8,128)}, u32[]{:S(2)}) %copy-start) | copy-done | bytes 20971544
  102.0 0.0 copy-start.1
  102.0 0.7 copy-done.1
  102.7 22.1 %combine.1 = (f32[16,16,32,128]{3,2,1,0:T(8,128)}, f32[16,16,32,128]{3,2,1,0:T(8,128)}) custom-call(f32[32,128]{1,0:T(8,128)S(1)} %copy-done.1, f32[5,16,32,16,128]{4,3,2,1,0:T(8,128)S(1)} %copy-done), custom_call_target="tpu_custom_call" | custom-call | tf_op jit(solution)/shard_map/combine/pallas_call | solution.py:375
Async XLA Ops:
  95.0 7.0 %copy-start = (f32[5,16,32,16,128]{4,3,2,1,0:T(8,128)S(1)}, f32[5,16,32,16,128]{4,3,2,1,0:T(8,128)}, u32[]{:S(2)}) copy-start(f32[5,16,32,16,128]{4,3,2,1,0:T(8,128)} %get-tuple-element.5.w_ref) | copy-start | bytes 62914564
  102.0 0.7 copy-start.1

commit v2 on v1

--- a/solution.py
+++ b/solution.py
@@ -10,6 +10,9 @@
 
 S = 16
 STEPS = 4
+PIECES = 4
+UNROLL = 2
+BLOCK = 4
 MESH = pl.DeviceIdType.MESH
 
 
@@ -75,10 +78,16 @@
         pl.when(jnp.logical_not(edges[side]))(functools.partial(zero_side, side))
     pl.semaphore_wait(barrier, nbx - 1 + nby - 1)
 
+    YP, XP = Y // PIECES, X // PIECES
+
     targets = ((bx - 1, by), (bx + 1, by), (bx, by - 1), (bx, by + 1))
 
-    def face_copies(ref, send, recv, side):
+    def face_copies(ref, send, recv, side, piece=None):
         xs, ys = pl.ds(1, X), pl.ds(1, Y)
+        if piece is not None:
+            send, recv = send.at[piece], recv.at[piece]
+            xs = pl.ds(1 + piece * XP, XP)
+            ys = pl.ds(1 + piece * YP, YP)
         src, dst = (
             (ref.at[1, ys], ref.at[X + 1, ys]),
             (ref.at[X, ys], ref.at[0, ys]),
@@ -90,28 +99,29 @@
             device_id=targets[side], device_id_type=MESH,
         )
 
-    def start_faces(ref, send, recv):
+    def start_faces(ref, send, recv, piece=None, sides=range(4)):
+        for side in sides:
+            @pl.when(edges[side])
+            def _(side=side):
+                face_copies(ref, send, recv, side, piece).start()
+
+    def wait_recv(ref, send, recv, piece=None, sides=range(4)):
+        for side in sides:
+            @pl.when(edges[side])
+            def _(side=side):
+                face_copies(ref, send, recv, side ^ 1, piece).wait_recv()
+
+    def wait_send(ref, send, recv, piece=None):
         for side in range(4):
             @pl.when(edges[side])
             def _(side=side):
-                face_copies(ref, send, recv, side).start()
-
-    def wait_recv(ref, send, recv):
-        for side in range(4):
-            @pl.when(edges[side])
-            def _(side=side):
-                face_copies(ref, send, recv, side ^ 1).wait_recv()
-
-    def wait_send(ref, send, recv):
-        for side in range(4):
-            @pl.when(edges[side])
-            def _(side=side):
-                face_copies(ref, send, recv, side).wait_send()
+                face_copies(ref, send, recv, side, piece).wait_send()
 
     start_faces(kp, k_send, k_recv)
     for c in loads:
         c.wait()
-    start_faces(v.at[0], h_send.at[0], h_recv.at[0])
+    for piece in [0, PIECES - 1] + list(range(1, PIECES - 1)):
+        start_faces(v.at[0], h_send.at[0], h_recv.at[0], piece)
     stores = [
         pltpu.make_async_copy(
             v.at[j, pl.ds(1, X), pl.ds(1, Y)], w_out.at[j], out_sem.at[j])
@@ -168,35 +178,28 @@
         else:
             v[j + 1, x, ys] = out - v[j - 1, x, ys]
 
-    CH = 4
-
-    def rows(j, x, lo, hi):
-        count = (hi - lo) // CH
-
-        @pl.loop(0, count)
-        def _(i):
-            stencil(j, x, lo + i * CH, CH)
-        if (hi - lo) % CH:
-            stencil(j, x, lo + count * CH, (hi - lo) % CH)
-
-    def boundary(j):
-        rows(j, 1, 1, Y + 1)
-        rows(j, X, 1, Y + 1)
-
-        @pl.loop(2, X)
+    def edge_y(j, piece):
+        first = 1 if piece > 0 else 2
+        last = (piece + 1) * XP + (1 if piece < PIECES - 1 else 0)
+
+        @pl.loop(first + piece * XP, last)
         def _(x):
             stencil(j, x, 1, 1)
             stencil(j, x, Y, 1)
 
-    def interior(j):
-        @pl.loop(2, X)
+    def edge_x(j, piece):
+        stencil(j, 1, 1 + piece * YP, YP)
+        stencil(j, X, 1 + piece * YP, YP)
+
+    def interior(j, lo, hi):
+        @pl.loop(lo, hi)
         def _(x):
-            rows(j, x, 2, Y)
+            stencil(j, x, 2, Y - 2)
 
     def flat(j, x):
         return jnp.concatenate([v[j, x, 1 + y] for y in range(Y)], axis=1)
 
-    def gram(j):
+    def gram(j, xlo, xhi, total):
         def body(x, total):
             hi, lo = split(flat(j, x))
             right = jnp.concatenate([hi, lo], axis=0)
@@ -208,7 +211,11 @@
                 left, right, (((1,), (1,)), ((), ())), preferred_element_type=jnp.float32)
 
         n = 32 if j == 0 else 64
-        total = lax.fori_loop(1, X + 1, body, jnp.zeros((n, 32), jnp.float32))
+        if total is None:
+            total = jnp.zeros((n, 32), jnp.float32)
+        return lax.fori_loop(xlo, xhi, body, total, unroll=UNROLL)
+
+    def keep(j, total):
         cols = total[:, :16] + total[:, 16:]
         same = cols[0:16] + cols[16:32]
         gl[0:16, 16 * j:16 * j + 16] = same
@@ -216,15 +223,36 @@
             gl[16:32, 16 * j:16 * j + 16] = cols[32:48] + cols[48:64]
 
     gl[...] = jnp.zeros_like(gl)
-    gram(0)
+    order = [0, PIECES - 1] + list(range(1, PIECES - 1))
+    keep(0, gram(0, 1, X + 1, None))
     for j in range(STEPS):
-        wait_recv(v.at[j], h_send.at[j], h_recv.at[j])
-        boundary(j)
-        if j + 1 < STEPS:
-            start_faces(v.at[j + 1], h_send.at[j + 1], h_recv.at[j + 1])
-        interior(j)
+        ref, send, recv = v.at[j], h_send.at[j], h_recv.at[j]
+        total = None
+        for at, piece in enumerate(order):
+            if at == 0:
+                wait_recv(ref, send, recv, 0, (2, 3))
+                wait_recv(ref, send, recv, PIECES - 1, (2, 3))
+            elif at > 1:
+                wait_recv(ref, send, recv, piece, (2, 3))
+            wait_recv(ref, send, recv, piece, (0, 1))
+            edge_x(j, piece)
+            edge_y(j, piece)
+            if j + 1 < STEPS:
+                nxt = (v.at[j + 1], h_send.at[j + 1], h_recv.at[j + 1])
+                start_faces(*nxt, piece, (0, 1))
+                if at == 1:
+                    start_faces(*nxt, 0, (2, 3))
+                    start_faces(*nxt, piece, (2, 3))
+                elif at > 1:
+                    start_faces(*nxt, piece, (2, 3))
+            lo = 1 + piece * XP
+            interior(j, max(lo, 2), min(lo + XP, X))
+            if j > 0:
+                total = gram(j, lo, lo + XP, total)
+        if j > 0:
+            keep(j, total)
         stores[j + 1].start()
-        gram(j + 1)
+    keep(STEPS, gram(STEPS, 1, X + 1, None))
 
     def spread(axis_at, n, own, src, slots, send, recv):
         copies = []
@@ -249,7 +277,8 @@
 
     wait_send(kp, k_send, k_recv)
     for j in range(STEPS):
-        wait_send(v.at[j], h_send.at[j], h_recv.at[j])
+        for piece in range(PIECES):
+            wait_send(v.at[j], h_send.at[j], h_recv.at[j], piece)
     for c in stores:
         c.wait()
 
@@ -317,16 +346,17 @@
         stacked = solve(g_ref[...])
         c_ref[...] = stacked.T[0:32].astype(jnp.bfloat16)
 
-    CH = 8
-
-    @pl.loop(0, Y // CH)
+    CH = 16
+
+    @pl.loop(0, BLOCK * (Y // CH))
     def _(t):
-        y0 = pl.multiple_of(t * CH, CH)
+        x = t // (Y // CH)
+        y0 = pl.multiple_of(lax.rem(t, Y // CH) * CH, CH)
         cols = []
         for y in range(CH):
             his, los = [], []
             for j in range(STEPS + 1):
-                hi, lo = split(w_ref[j, 0, y0 + y])
+                hi, lo = split(w_ref[j, x, y0 + y])
                 his.append(hi)
                 los.append(lo)
             cols.append(jnp.concatenate(
@@ -335,8 +365,8 @@
         out = jnp.dot(c_ref[...], right, preferred_element_type=jnp.float32)
         out = jnp.stack([out[:, 128 * y:128 * y + 128] for y in range(CH)], axis=0)
         out = jnp.swapaxes(out, 0, 1)
-        sol_ref[:, 0, pl.ds(y0, CH)] = out[0:16]
-        res_ref[:, 0, pl.ds(y0, CH)] = out[16:32]
+        sol_ref[:, x, pl.ds(y0, CH)] = out[0:16]
+        res_ref[:, x, pl.ds(y0, CH)] = out[16:32]
 
 
 def shards(right_side, conductivity):
@@ -364,7 +394,7 @@
             pltpu.VMEM((nbx, 32, 128), f32),
             pltpu.VMEM((nby, 32, 128), f32),
             dma((S,)), dma((STEPS + 1,)), dma((4,)), dma((4,)),
-            dma((STEPS, 4)), dma((STEPS, 4)),
+            dma((STEPS, PIECES, 4)), dma((STEPS, PIECES, 4)),
             dma((nbx,)), dma((nbx,)), dma((nby,)), dma((nby,)),
         ],
         compiler_params=pltpu.CompilerParams(
@@ -374,18 +404,18 @@
     out = jax.ShapeDtypeStruct((S, X, Y, Z), f32)
     return pl.pallas_call(
         functools.partial(combine_kernel, Y),
-        grid=(X,),
+        grid=(X // BLOCK,),
         out_shape=(out, out),
         in_specs=[
             pl.BlockSpec((32, 128), lambda x: (0, 0)),
-            pl.BlockSpec((STEPS + 1, 1, Y, S, Z), lambda x: (0, x, 0, 0, 0)),
+            pl.BlockSpec((STEPS + 1, BLOCK, Y, S, Z), lambda x: (0, x, 0, 0, 0)),
         ],
         out_specs=(
-            pl.BlockSpec((S, 1, Y, Z), lambda x: (0, x, 0, 0)),
-            pl.BlockSpec((S, 1, Y, Z), lambda x: (0, x, 0, 0)),
+            pl.BlockSpec((S, BLOCK, Y, Z), lambda x: (0, x, 0, 0)),
+            pl.BlockSpec((S, BLOCK, Y, Z), lambda x: (0, x, 0, 0)),
         ),
         scratch_shapes=[pltpu.VMEM((32, 256), jnp.bfloat16)],
-        compiler_params=pltpu.CompilerParams(vmem_limit_bytes=32 * 1024 * 1024),
+        compiler_params=pltpu.CompilerParams(vmem_limit_bytes=58 * 1024 * 1024),
         name="combine",
     )(g, w)
 

time: 125 us -> 82 us (0.66)
  Pallas kernels: 116 us -> 81.1 us
  local copies, waits for them, and re-layouts: 7.67 us -> 0 us
    pallas_call x1, Pallas kernels: 94.4 us -> 60.7 us  [shards(): pl.pallas_call(functools.partial(basis_kernel, nbx, nby, X, Y), out_shape...]
    unnamed x4 -> x0, local copies, waits for them, and re-layouts: 7.67 us -> none
    pallas_call x1, Pallas kernels: 22.1 us -> 20.4 us  [shards(): pl.pallas_call(functools.partial(combine_kernel, Y), grid=(X // BLOCK,),...]
where the time goes in v2:
time: 82 us; the launch traced here: 81.8 us
  Pallas kernels  81.1 us (99%)
    pallas_call x1, Pallas kernels, shards(): pl.pallas_call(functools.partial(basis_kernel, nbx, nby, X, Y), out_shape...  60.7 us
    pallas_call x1, Pallas kernels, shards(): pl.pallas_call(functools.partial(combine_kernel, Y), grid=(X // BLOCK,),...  20.4 us

profile of v2, /device:TPU:0, one launch (start us, length us, event | category | flops | bytes accessed | tf_op | source)
XLA Modules:
  0.0 81.8 jit_solution(1582685668750926425)
XLA Ops:
  0.6 60.7 %basis.1 = (f32[5,16,32,16,128]{4,3,2,1,0:T(8,128)}, f32[32,128]{1,0:T(8,128)}) custom-call(f32[16,16,32,128]{3,2,1,0:T(8,128)} %rhs.1, f32[16,32,1,128]{3,2,1,0:T(1,128)} %bitcast.1), custom_call_target="tpu_custom_call" | custom-call | tf_op jit(solution)/shard_map/basis/pallas_call | solution.py:377
  61.4 20.4 %combine.1 = (f32[16,16,32,128]{3,2,1,0:T(8,128)}, f32[16,16,32,128]{3,2,1,0:T(8,128)}) custom-call(f32[32,128]{1,0:T(8,128)} %get-tuple-element.4.g_ref, f32[5,16,32,16,128]{4,3,2,1,0:T(8,128)} %get-tuple-element.5.w_ref), custom_call_target="tpu_custom_call" | custom-call | tf_op jit(solution)/shard_map/combine/pallas_call | solution.py:405

commit v3 on v2

--- a/solution.py
+++ b/solution.py
@@ -317,10 +317,17 @@
     a = jnp.concatenate(rows, axis=0)
     order = S * STEPS
     place = lax.broadcasted_iota(jnp.int32, (order, 128), 0)
-    for p in range(order):
-        col = jnp.broadcast_to(a[:, p:p + 1], (order, 128))
-        row = jnp.broadcast_to(a[p:p + 1] / col[p:p + 1], (order, 128))
-        a = jnp.where(place == p, row, a - col * row)
+    for p in range(0, order, 2):
+        one = jnp.broadcast_to(a[:, p:p + 1], (order, 128))
+        two = jnp.broadcast_to(a[:, p + 1:p + 2], (order, 128))
+        inverse = 1.0 / one[p:p + 1]
+        first = a[p:p + 1] * inverse
+        low = one[p + 1:p + 2]
+        high = two[p:p + 1] * inverse
+        second = (a[p + 1:p + 2] - low * first) / (two[p + 1:p + 2] - low * high)
+        first = first - high * second
+        rest = a - one * first - two * second
+        a = jnp.where(place == p, first, jnp.where(place == p + 1, second, rest))
     coeffs = [a[16 * i:16 * i + 16, order:order + 16] for i in range(STEPS)]
     zero = jnp.zeros((16, 16), jnp.float32)
     eye = jnp.where(

time: 82 us -> 80.3 us (0.979)
  Pallas kernels: 81.1 us -> 79.4 us
    pallas_call x1, Pallas kernels: 20.4 us -> 18.7 us  [shards(): pl.pallas_call(functools.partial(combine_kernel, Y), grid=(X // BLOCK,),...]
where the time goes in v3:
time: 80.3 us; the launch traced here: 80.1 us
  Pallas kernels  79.4 us (99%)
    pallas_call x1, Pallas kernels, shards(): pl.pallas_call(functools.partial(basis_kernel, nbx, nby, X, Y), out_shape...  60.7 us
    pallas_call x1, Pallas kernels, shards(): pl.pallas_call(functools.partial(combine_kernel, Y), grid=(X // BLOCK,),...  18.7 us

profile of v3, /device:TPU:0, one launch (start us, length us, event | category | flops | bytes accessed | tf_op | source)
XLA Modules:
  0.0 80.1 jit_solution(16051255669057305592)
XLA Ops:
  0.6 60.7 %basis.1 = (f32[5,16,32,16,128]{4,3,2,1,0:T(8,128)}, f32[32,128]{1,0:T(8,128)}) custom-call(f32[16,16,32,128]{3,2,1,0:T(8,128)} %rhs.1, f32[16,32,1,128]{3,2,1,0:T(1,128)} %bitcast.1), custom_call_target="tpu_custom_call" | custom-call | tf_op jit(solution)/shard_map/basis/pallas_call | solution.py:384
  61.4 18.7 %combine.1 = (f32[16,16,32,128]{3,2,1,0:T(8,128)}, f32[16,16,32,128]{3,2,1,0:T(8,128)}) custom-call(f32[32,128]{1,0:T(8,128)} %get-tuple-element.4.g_ref, f32[5,16,32,16,128]{4,3,2,1,0:T(8,128)} %get-tuple-element.5.w_ref), custom_call_target="tpu_custom_call" | custom-call | tf_op jit(solution)/shard_map/combine/pallas_call | solution.py:412
